TPU v7x, 128 devices: a whole 4x4x4 slice. The times are simulated.
128 devices in a mesh: rep: 2 (over x_hi), shard: 64 (over z, x_lo, y, core).
Axes of the slice: x: 4 (x_hi: 2, x_lo: 2; x = x_hi * 2 + x_lo), y: 4, z: 4, core: 2. Of those that a mesh axis runs over, the one named last changes fastest.
Arguments:
- tokens: bfloat16 [16384, 2048], P(('rep', 'shard')), may hold values from -6 to 6
- cotangent: bfloat16 [16384, 2048], P(('rep', 'shard')), may hold values from -6 to 6
- segments: int32 [128, 128], P(('rep', 'shard')), may hold values from 0 to 15, never falling along the last dimension, each value on 1 to 64 neighbouring positions
- project_in: float32 [2048, 3072], P('shard'), may hold values from -0.125 to 0.125
- project_out: float32 [2048, 2048], P('shard'), may hold values from -0.5 to 0.5
- gate_up: float32 [2, 2048, 8192], P(None, None, 'shard'), may hold values from -0.125 to 0.125
- down_weight: float32 [8192, 2048], P('shard'), may hold values from -0.125 to 0.125
- norm_gains: float32 [2, 2048], P(None, 'shard'), may hold values from 0.1 to 1.9
- first_in: float32 [2048, 3072], P('shard'), may hold values from -80 to 80
- first_out: float32 [2048, 2048], P('shard'), may hold values from -80 to 80
- first_gate: float32 [2, 2048, 8192], P(None, None, 'shard'), may hold values from -80 to 80
- first_down: float32 [8192, 2048], P('shard'), may hold values from -80 to 80
- first_gains: float32 [2, 2048], P(None, 'shard'), may hold values from -256 to 256
- second_in: float32 [2048, 3072], P('shard'), may hold values from 901.12 to 3604.48
- second_out: float32 [2048, 2048], P('shard'), may hold values from 901.12 to 3604.48
- second_gate: float32 [2, 2048, 8192], P(None, None, 'shard'), may hold values from 901.12 to 3604.48
- second_down: float32 [8192, 2048], P('shard'), may hold values from 901.12 to 3604.48
- second_gains: float32 [2, 2048], P(None, 'shard'), may hold values from 8192 to 32768
Outputs:
- layer_out: float32 [16384, 2048], P(('rep', 'shard'))
- input_grad: float32 [16384, 2048], P(('rep', 'shard'))
- new_in: float32 [2048, 3072], P('shard')
- new_out: float32 [2048, 2048], P('shard')
- new_gate: float32 [2, 2048, 8192], P(None, None, 'shard')
- new_down: float32 [8192, 2048], P('shard')
- new_gains: float32 [2, 2048], P(None, 'shard')
- moment_in: float32 [2048, 3072], P('shard')
- moment_out: float32 [2048, 2048], P('shard')
- moment_gate: float32 [2, 2048, 8192], P(None, None, 'shard')
- moment_down: float32 [8192, 2048], P('shard')
- moment_gains: float32 [2, 2048], P(None, 'shard')
- square_in: float32 [2048, 3072], P('shard')
- square_out: float32 [2048, 2048], P('shard')
- square_gate: float32 [2, 2048, 8192], P(None, None, 'shard')
- square_down: float32 [8192, 2048], P('shard')
- square_gains: float32 [2, 2048], P(None, 'shard')
Inputs may be any that keep to these rules, and one draw needn't show every extreme that they name: `segments`: within each sequence the document numbers never fall and start at 0; every document holds 1 to 64 tokens, and one of each sequence holds exactly 64.
All inputs are finite; a program needn't handle non-finite values.
Results may differ from a plain program's by a relative error of at most 0.02.
Values may be sent and summed in bfloat16 or wider, within the bound.
No kernel may reach another device: no remote copies, remote signals or barrier semaphores. Data moves between devices by JAX's collectives and lax.ppermute only.
A program may use at most 576 MiB of HBM per device.

v0:
```python
import jax
import jax.numpy as jnp
from jax import lax
from jax.sharding import PartitionSpec as P

HEADS = 32
KV_HEADS = 8
HEAD_DIM = 64
STEP = 10


eps_norm = 1e-05
rope_base = 500000.0
beta_one = 0.9
beta_two = 0.95
adam_eps = 1e-08
rate_matrix = 0.1
rate_gain = 1.0
decay_matrix = 0.1


def positions_of(segments):
    seq_len = segments.shape[-1]
    token_index = jnp.arange(seq_len, dtype=jnp.int32)
    changes = jnp.concatenate(
        [
            jnp.ones_like(segments[..., :1]),
            (segments[..., 1:] != segments[..., :-1]).astype(jnp.int32),
        ],
        axis=-1,
    )
    starts = jnp.where(changes > 0, token_index, 0)
    return token_index - lax.cummax(starts, axis=segments.ndim - 1)


def rotate(vectors, position, turn_sign):
    half_dim = vectors.shape[-1] // 2
    frequency = rope_base ** (-jnp.arange(half_dim, dtype=jnp.float32) * 2.0 / vectors.shape[-1])
    angles = position.astype(jnp.float32)[..., None] * frequency
    cosine = jnp.cos(angles)[..., None, :]
    sine_part = turn_sign * jnp.sin(angles)[..., None, :]
    first_half = vectors[..., :half_dim]
    second_half = vectors[..., half_dim:]
    return jnp.concatenate(
        [
            first_half * cosine - second_half * sine_part,
            second_half * cosine + first_half * sine_part,
        ],
        axis=-1,
    )


def normalize(values):
    inverse = lax.rsqrt(jnp.mean(values * values, axis=-1, keepdims=True) + eps_norm)
    return (values * inverse, inverse)


def norm_back(grad_unit, unit_rows, inverse):
    return inverse * (
        grad_unit - unit_rows * jnp.mean(grad_unit * unit_rows, axis=-1, keepdims=True)
    )


def attention_core(queries, key_rows, values, allowed):
    score_scale = queries.shape[-1] ** (-0.5)
    scores = (
        jnp.einsum("akgd,ckd->kgac", queries, key_rows, preferred_element_type=jnp.float32)
        * score_scale
    )
    scores = jnp.where(allowed, scores, -1e30)
    row_top = jnp.max(scores, axis=-1, keepdims=True)
    row_exp = jnp.exp(scores - row_top)
    row_total = jnp.sum(row_exp, axis=-1, keepdims=True)
    soft_probs = row_exp / row_total
    logsum = row_top + jnp.log(row_total)
    attended = jnp.einsum(
        "kgac,ckd->akgd",
        soft_probs.astype(jnp.bfloat16),
        values,
        preferred_element_type=jnp.float32,
    )
    return (attended, logsum)


def attention_back(queries, key_rows, values, allowed, logsum, grad_attended):
    score_scale = queries.shape[-1] ** (-0.5)
    scores = (
        jnp.einsum("akgd,ckd->kgac", queries, key_rows, preferred_element_type=jnp.float32)
        * score_scale
    )
    soft_probs = jnp.exp(jnp.where(allowed, scores, -1e30) - logsum)
    grad_values = jnp.einsum(
        "kgac,akgd->ckd",
        soft_probs.astype(jnp.bfloat16),
        grad_attended,
        preferred_element_type=jnp.float32,
    )
    grad_probs = jnp.einsum(
        "akgd,ckd->kgac", grad_attended, values, preferred_element_type=jnp.float32
    )
    row_inner = jnp.sum(soft_probs * grad_probs, axis=-1, keepdims=True)
    grad_scores = (soft_probs * (grad_probs - row_inner)).astype(jnp.bfloat16)
    grad_queries = (
        jnp.einsum("kgac,ckd->akgd", grad_scores, key_rows, preferred_element_type=jnp.float32)
        * score_scale
    )
    grad_keys = (
        jnp.einsum("kgac,akgd->ckd", grad_scores, queries, preferred_element_type=jnp.float32)
        * score_scale
    )
    return (grad_queries, grad_keys, grad_values)


def adam_update(master, gradient, moment_old, square_old, step_rate, decay_rate):
    moment_new = beta_one * moment_old + (1.0 - beta_one) * gradient
    square_new = beta_two * square_old + (1.0 - beta_two) * gradient * gradient
    moment_hat = moment_new / (1.0 - beta_one**STEP)
    square_hat = square_new / (1.0 - beta_two**STEP)
    updated = master - step_rate * (
        moment_hat / (jnp.sqrt(square_hat) + adam_eps) + decay_rate * master
    )
    return (updated, moment_new, square_new)


def left_dot(left_rows, right_rows):
    return lax.dot_general(
        left_rows, right_rows, (((0,), (0,)), ((), ())), preferred_element_type=jnp.float32
    )


def right_dot(left_rows, right_rows):
    return lax.dot_general(
        left_rows, right_rows, (((1,), (1,)), ((), ())), preferred_element_type=jnp.float32
    )


def gate_backward(grad_act, gate_pre, up_pre):
    sigmoid_gate = jax.nn.sigmoid(gate_pre)
    grad_gate = (grad_act * up_pre * sigmoid_gate * (1.0 + gate_pre * (1.0 - sigmoid_gate))).astype(
        jnp.bfloat16
    )
    grad_up = (grad_act * gate_pre * sigmoid_gate).astype(jnp.bfloat16)
    return (grad_gate, grad_up)


def unit_rows(column_part, token_part, start, count):
    return left_dot(column_part, token_part)


def local(
    tokens,
    cotangent,
    segments,
    project_in,
    project_out,
    gate_up,
    down_weight,
    norm_gains,
    first_in,
    first_out,
    first_gate,
    first_down,
    first_gains,
    second_in,
    second_out,
    second_gate,
    second_down,
    second_gains,
):
    seq_len = tokens.shape[0]
    group_size = HEADS // KV_HEADS
    query_width = HEADS * HEAD_DIM
    kv_width = KV_HEADS * HEAD_DIM
    inputs = tokens.astype(jnp.float32)
    grad_out = cotangent.astype(jnp.float32)
    position = positions_of(segments)[0]
    seg_row = segments[0]
    token_index = jnp.arange(seq_len, dtype=jnp.int32)
    allowed = (seg_row[:, None] == seg_row[None, :]) & (
        token_index[:, None] >= token_index[None, :]
    )
    full_in, full_out, gains_low = (
        lax.all_gather(project_in.astype(jnp.bfloat16), "shard", axis=0, tiled=True),
        lax.all_gather(project_out.astype(jnp.bfloat16), "shard", axis=0, tiled=True),
        lax.all_gather(norm_gains.astype(jnp.bfloat16), "shard", axis=1, tiled=True),
    )
    gain_one = gains_low[0].astype(jnp.float32)
    gain_two = gains_low[1].astype(jnp.float32)
    unit_one, inverse_one = normalize(inputs)
    normed_one = (unit_one * gain_one).astype(jnp.bfloat16)
    mixed_in = jnp.dot(normed_one, full_in, preferred_element_type=jnp.float32)
    query_raw = mixed_in[:, :query_width].reshape(seq_len, HEADS, HEAD_DIM)
    key_raw = mixed_in[:, query_width : query_width + kv_width].reshape(seq_len, KV_HEADS, HEAD_DIM)
    value_raw = mixed_in[:, query_width + kv_width :].reshape(seq_len, KV_HEADS, HEAD_DIM)
    queries = (
        rotate(query_raw, position, 1.0)
        .astype(jnp.bfloat16)
        .reshape(seq_len, KV_HEADS, group_size, HEAD_DIM)
    )
    key_rows = rotate(key_raw, position, 1.0).astype(jnp.bfloat16)
    values = value_raw.astype(jnp.bfloat16)
    attended, logsum = attention_core(queries, key_rows, values, allowed)
    attended_low = attended.reshape(seq_len, query_width).astype(jnp.bfloat16)
    hidden = inputs + jnp.dot(attended_low, full_out, preferred_element_type=jnp.float32)
    unit_two, inverse_two = normalize(hidden)
    normed_two = (unit_two * gain_two).astype(jnp.bfloat16)
    gate_full, down_full = (
        lax.all_gather(gate_up.astype(jnp.bfloat16), "shard", axis=2, tiled=True),
        lax.all_gather(down_weight.astype(jnp.bfloat16), "shard", axis=0, tiled=True),
    )
    gate_pre = jnp.dot(normed_two, gate_full[0], preferred_element_type=jnp.float32)
    up_pre = jnp.dot(normed_two, gate_full[1], preferred_element_type=jnp.float32)
    activated = (jax.nn.silu(gate_pre) * up_pre).astype(jnp.bfloat16)
    layer_out = hidden + jnp.dot(activated, down_full, preferred_element_type=jnp.float32)
    gate_back, down_back = (
        lax.all_gather(gate_up.astype(jnp.bfloat16), "shard", axis=2, tiled=True),
        lax.all_gather(down_weight.astype(jnp.bfloat16), "shard", axis=0, tiled=True),
    )
    grad_act = right_dot(cotangent, down_back)
    grad_gate, grad_up = gate_backward(grad_act, gate_pre, up_pre)
    grad_normed_two = right_dot(grad_gate, gate_back[0]) + right_dot(grad_up, gate_back[1])
    owned_parts = []
    for column_part, token_part in (
        (grad_gate, normed_two),
        (grad_up, normed_two),
        (activated, cotangent),
    ):
        owned_parts.append(
            lax.psum_scatter(
                unit_rows(
                    column_part, token_part, jnp.int32(0), lax.axis_size("shard") * gate_up.shape[2]
                ),
                "shard",
                scatter_dimension=0,
                tiled=True,
            )
        )
    own_gate = jnp.stack([owned_parts[0].T, owned_parts[1].T])
    own_down = owned_parts[2]
    grad_gain_two = jnp.sum(grad_normed_two * unit_two, axis=0)
    grad_hidden = grad_out + norm_back(grad_normed_two * gain_two, unit_two, inverse_two)
    grad_branch = grad_hidden.astype(jnp.bfloat16)
    back_in, back_out = (
        lax.all_gather(project_in.astype(jnp.bfloat16), "shard", axis=0, tiled=True),
        lax.all_gather(project_out.astype(jnp.bfloat16), "shard", axis=0, tiled=True),
    )
    term_out = left_dot(attended_low, grad_branch)
    grad_attended = (
        right_dot(grad_branch, back_out)
        .astype(jnp.bfloat16)
        .reshape(seq_len, KV_HEADS, group_size, HEAD_DIM)
    )
    grad_queries, grad_keys, grad_values = attention_back(
        queries, key_rows, values, allowed, logsum, grad_attended
    )
    grad_query_raw = rotate(grad_queries.reshape(seq_len, HEADS, HEAD_DIM), position, -1.0)
    grad_key_raw = rotate(grad_keys, position, -1.0)
    grad_mixed = jnp.concatenate(
        [
            grad_query_raw.reshape(seq_len, query_width),
            grad_key_raw.reshape(seq_len, kv_width),
            grad_values.reshape(seq_len, kv_width),
        ],
        axis=1,
    ).astype(jnp.bfloat16)
    term_in = left_dot(normed_one, grad_mixed)
    grad_normed_one = right_dot(grad_mixed, back_in)
    grad_gain_one = jnp.sum(grad_normed_one * unit_one, axis=0)
    input_grad = grad_hidden + norm_back(grad_normed_one * gain_one, unit_one, inverse_one)
    term_gains = jnp.stack([grad_gain_one, grad_gain_two])
    own_in, own_out, own_gains = (
        lax.psum_scatter(term_in, "shard", scatter_dimension=0, tiled=True),
        lax.psum_scatter(term_out, "shard", scatter_dimension=0, tiled=True),
        lax.psum_scatter(term_gains, "shard", scatter_dimension=1, tiled=True),
    )
    sum_in, sum_out, sum_gate, sum_down, sum_gains = (
        lax.psum(own_in.astype(jnp.bfloat16), "rep").astype(jnp.float32),
        lax.psum(own_out.astype(jnp.bfloat16), "rep").astype(jnp.float32),
        lax.psum(own_gate.astype(jnp.bfloat16), "rep").astype(jnp.float32),
        lax.psum(own_down.astype(jnp.bfloat16), "rep").astype(jnp.float32),
        lax.psum(own_gains.astype(jnp.bfloat16), "rep").astype(jnp.float32),
    )
    new_in, moment_in, square_in = adam_update(
        project_in, sum_in, first_in, second_in, rate_matrix, decay_matrix
    )
    new_out, moment_out, square_out = adam_update(
        project_out, sum_out, first_out, second_out, rate_matrix, decay_matrix
    )
    new_gate, moment_gate, square_gate = adam_update(
        gate_up, sum_gate, first_gate, second_gate, rate_matrix, decay_matrix
    )
    new_down, moment_down, square_down = adam_update(
        down_weight, sum_down, first_down, second_down, rate_matrix, decay_matrix
    )
    new_gains, moment_gains, square_gains = adam_update(
        norm_gains, sum_gains, first_gains, second_gains, rate_gain, 0.0
    )
    return (
        layer_out,
        input_grad,
        new_in,
        new_out,
        new_gate,
        new_down,
        new_gains,
        moment_in,
        moment_out,
        moment_gate,
        moment_down,
        moment_gains,
        square_in,
        square_out,
        square_gate,
        square_down,
        square_gains,
    )


def solution(mesh):
    in_specs = (
        P(("rep", "shard"), None),
        P(("rep", "shard"), None),
        P(("rep", "shard"), None),
        P("shard", None),
        P("shard", None),
        P(None, None, "shard"),
        P("shard", None),
        P(None, "shard"),
        P("shard", None),
        P("shard", None),
        P(None, None, "shard"),
        P("shard", None),
        P(None, "shard"),
        P("shard", None),
        P("shard", None),
        P(None, None, "shard"),
        P("shard", None),
        P(None, "shard"),
    )
    out_specs = (
        P(("rep", "shard"), None),
        P(("rep", "shard"), None),
        P("shard", None),
        P("shard", None),
        P(None, None, "shard"),
        P("shard", None),
        P(None, "shard"),
        P("shard", None),
        P("shard", None),
        P(None, None, "shard"),
        P("shard", None),
        P(None, "shard"),
        P("shard", None),
        P("shard", None),
        P(None, None, "shard"),
        P("shard", None),
        P(None, "shard"),
    )
    return jax.shard_map(local, mesh=mesh, in_specs=in_specs, out_specs=out_specs, check_vma=False)
```

profile of v0, /device:TPU:24, one launch (start us, length us, event | category | flops | bytes accessed | tf_op | source)
XLA Modules:
  0.0 3130.2 jit_solution(17457224329896774449)
XLA Ops:
  14.5 73.1 %all-gather = bf16[64,32,2]{1,2,0:T(2,128)(2,1)S(1)} all-gather(bf16[1,32,2]{1,2,0:T(2,128)(2,1)S(1)} %convert_bitcast_fusion.2), channel_id=1, replica_groups=mesh['rep'=2,'shard'=64] {'shard'}, dimensions={0}, use_global_device_ids=true | all-gather | bytes 8320 | tf_op jit(solution)/shard_map/all_gather | solution.py:185
  89.4 40.0 %all-gather.6.cloned.1.call-done = bf16[2048,3072]{1,0:T(8,128)(2,1)} async-done(((bf16[32,3072]{1,0:T(8,128)(2,1)}), bf16[2048,3072]{1,0:T(8,128)(2,1)}) %all-gather.6.cloned.1.call-update) | async-done | bytes 12582928 | tf_op jit(solution)/shard_map/all_gather | solution.py:183
  139.0 103.2 %all-gather.8.cloned.1.call-done = bf16[2048,2048]{1,0:T(8,128)(2,1)} async-done(((bf16[32,2048]{1,0:T(8,128)(2,1)}), bf16[2048,2048]{1,0:T(8,128)(2,1)}) %all-gather.8.cloned.1.call-update) | async-done | bytes 8388624 | tf_op jit(solution)/shard_map/all_gather | solution.py:184
  248.1 389.3 %all-gather.10.cloned.1.call-done = bf16[2,2048,8192]{2,1,0:T(8,128)(2,1)} async-done(((bf16[2,2048,128]{2,1,0:T(8,128)(2,1)}), bf16[2,2048,8192]{2,1,0:T(8,128)(2,1)}) %all-gather.10.cloned.1.call-update) | async-done | bytes 67108880 | tf_op jit(solution)/shard_map/all_gather | solution.py:208
  637.4 15.4 fusion.1
  652.8 15.5 fusion.3
  668.4 160.3 %all-gather.12.cloned.1.call-done = bf16[8192,2048]{1,0:T(8,128)(2,1)} async-done(((bf16[128,2048]{1,0:T(8,128)(2,1)}), bf16[8192,2048]{1,0:T(8,128)(2,1)}) %all-gather.12.cloned.1.call-update) | async-done | bytes 33554448 | tf_op jit(solution)/shard_map/all_gather | solution.py:209
  828.7 20.9 multiply_convert_fusion
  849.6 17.3 fusion
  866.9 20.2 multiply_reduce_fusion
  890.8 8.1 fusion.36
  915.1 11.2 fusion.32
  927.9 23.7 fusion.62
  953.2 23.6 fusion.61
  978.5 23.5 fusion.63
  1011.5 9.3 fusion.25
  1023.6 169.5 %reduce-scatter.11.cloned.1.call-done = f32[32,2048]{1,0:T(8,128)} async-done(((f32[2048,2048]{1,0:T(8,128)}), f32[32,2048]{1,0:T(8,128)}) %reduce-scatter.11.cloned.1.call-update) | async-done | bytes 262160 | tf_op jit(solution)/shard_map/reduce_scatter | solution.py:273
  1194.7 324.2 %reduce-scatter.9.cloned.1.call-done = f32[32,3072]{1,0:T(8,128)} async-done(((f32[2048,3072]{1,0:T(8,128)}), f32[32,3072]{1,0:T(8,128)}) %reduce-scatter.9.cloned.1.call-update) | async-done | bytes 393232 | tf_op jit(solution)/shard_map/reduce_scatter | solution.py:272
  1520.6 398.2 %reduce-scatter.15.cloned.1.call-done = f32[128,2048]{1,0:T(8,128)} async-done(((f32[8192,2048]{1,0:T(8,128)}), f32[128,2048]{1,0:T(8,128)}) %reduce-scatter.15.cloned.1.call-update) | async-done | bytes 1048592 | tf_op jit(solution)/shard_map/reduce_scatter | solution.py:229
  1920.1 403.3 %reduce-scatter.13.cloned.1.call-done = f32[128,2048]{1,0:T(8,128)} async-done(((f32[8192,2048]{1,0:T(8,128)}), f32[128,2048]{1,0:T(8,128)}) %reduce-scatter.13.cloned.1.call-update) | async-done | bytes 1048592 | tf_op jit(solution)/shard_map/reduce_scatter | solution.py:229
  2325.8 402.2 %reduce-scatter.17.cloned.1.call-done = f32[128,2048]{1,0:T(8,128)} async-done(((f32[8192,2048]{1,0:T(8,128)}), f32[128,2048]{1,0:T(8,128)}) %reduce-scatter.17.cloned.1.call-update) | async-done | bytes 1048592 | tf_op jit(solution)/shard_map/reduce_scatter | solution.py:229
  2730.2 14.0 convolution_add_fusion
  2744.2 273.6 %reduce-scatter.19.cloned.1.call-done = f32[32,2]{1,0:T(8,128)} async-done(((f32[2048,2]{1,0:T(8,128)}), f32[32,2]{1,0:T(8,128)}) %reduce-scatter.19.cloned.1.call-update) | async-done | bytes 272
  3025.6 76.8 %all-reduce.3.cloned.1.call-done = (bf16[32,3072]{1,0:T(8,128)(2,1)}, bf16[32,2048]{1,0:T(8,128)(2,1)}, bf16[2,2048,128]{1,2,0:T(8,128)(2,1)}, bf16[128,2048]{1,0:T(8,128)(2,1)}) async-done(((bf16[32,3072]{1,0:T(8,128)(2,1)}, bf16[32,2048]{1,0:T(8,128)(2,1)}, bf16[2,2048,128]{1,2,0:T(8,128)(2,1)}, bf16[128,2048]{1,0:T(8,128)(2,1)}), (bf16[32,3072]{1,0:T(8,128)(2,1)}, bf16[32,2048]{1,0:T(8,128)(2,1)}, ...) | async-done | bytes 1900560 | tf_op jit(solution)/shard_map/psum | solution.py:277
  (189 shorter events, 98.9 us)
Async XLA Ops:
  7.2 122.2 %all-gather.6.cloned.1.call-start = ((), (), s32[]{:S(2)}) async-start(), calls=%async_computation.6 | async-start | bytes 12779520 | tf_op jit(solution)/shard_map/all_gather | solution.py:183
  9.0 233.2 %all-gather.8.cloned.1.call-start = ((), (), s32[]{:S(2)}) async-start(), calls=%async_computation.7 | async-start | bytes 8519680 | tf_op jit(solution)/shard_map/all_gather | solution.py:184
  10.7 626.7 %all-gather.10.cloned.1.call-start = ((), (), s32[]{:S(2)}) async-start(), calls=%async_computation.8 | async-start | bytes 68157440 | tf_op jit(solution)/shard_map/all_gather | solution.py:208
  13.5 74.2 %copy-start.43 = (s32[1,128]{1,0:T(1,128)S(1)}, s32[1,128]{1,0:T(1,128)}, u32[]{:S(2)}) copy-start(s32[1,128]{1,0:T(1,128)} %param.20) | copy-start | bytes 1540
  13.5 74.8 %copy-start = (bf16[128,2048]{1,0:T(8,128)(2,1)S(1)}, bf16[128,2048]{1,0:T(8,128)(2,1)}, u32[]{:S(2)}) copy-start(bf16[128,2048]{1,0:T(8,128)(2,1)} %param.18) | copy-start | bytes 1572868
  13.5 815.2 %all-gather.12.cloned.1.call-start = ((), (), s32[]{:S(2)}) async-start(), calls=%async_computation.9 | async-start | bytes 34078720 | tf_op jit(solution)/shard_map/all_gather | solution.py:209
  14.5 1178.6 %reduce-scatter.11.cloned.1.call-start = ((), (), s32[]{:S(2)}) async-start(), calls=%async_computation.11 | async-start | bytes 17039360 | tf_op jit(solution)/shard_map/reduce_scatter | solution.py:273
  88.5 47.4 %copy-start.39 = (f32[128]{0:T(128)}, f32[128]{0:T(128)S(1)}, u32[]{:S(2)}) copy-start(f32[128]{0:T(128)S(1)} %add_rsqrt_fusion.1) | copy-start | bytes 1540
  89.4 47.3 %copy-start.25 = (f32[128,32]{0,1:T(8,128)}, f32[128,32]{0,1:T(8,128)S(1)}, u32[]{:S(2)}) copy-start(f32[128,32]{0,1:T(8,128)S(1)} %get-tuple-element.106) | copy-start | bytes 49156
  139.0 108.0 %copy-start.9 = (bf16[8,64,4,128]{3,1,2,0:T(8,128)(2,1)}, bf16[8,64,4,128]{3,1,2,0:T(8,128)(2,1)S(1)}, u32[]{:S(2)}) copy-start(bf16[8,64,4,128]{3,1,2,0:T(8,128)(2,1)S(1)} %convolution_convert_fusion.1) | copy-start | bytes 1572868
  898.9 620.0 %reduce-scatter.9.cloned.1.call-start = ((), (), s32[]{:S(2)}) async-start(), calls=%async_computation.10 | async-start | bytes 25559040 | tf_op jit(solution)/shard_map/reduce_scatter | solution.py:272
  926.3 992.5 %reduce-scatter.15.cloned.1.call-start = ((), (), s32[]{:S(2)}) async-start(), calls=%async_computation.13 | async-start | bytes 68157440 | tf_op jit(solution)/shard_map/reduce_scatter | solution.py:229
  951.6 1371.8 %reduce-scatter.13.cloned.1.call-start = ((), (), s32[]{:S(2)}) async-start(), calls=%async_computation.12 | async-start | bytes 68157440 | tf_op jit(solution)/shard_map/reduce_scatter | solution.py:229
  976.8 1751.2 %reduce-scatter.17.cloned.1.call-start = ((), (), s32[]{:S(2)}) async-start(), calls=%async_computation.14 | async-start | bytes 68157440 | tf_op jit(solution)/shard_map/reduce_scatter | solution.py:229
  1002.0 2015.8 %reduce-scatter.19.cloned.1.call-start = ((), (), s32[]{:S(2)}) async-start(), calls=%async_computation.15 | async-start | bytes 1064960
  1011.5 9.3 copy-start.41
  1011.5 10.7 copy-start.2
  1023.5 2078.8 %all-reduce.3.cloned.1.call-start = ((), (), s32[]{:S(2)}) async-start(), calls=%async_computation.16 | async-start | bytes 3801088 | tf_op jit(solution)/shard_map/psum | solution.py:277
  2325.8 404.4 %copy-start.4 = (f32[128,2048]{1,0:T(8,128)S(1)}, f32[128,2048]{1,0:T(8,128)}, u32[]{:S(2)}) copy-start(f32[128,2048]{1,0:T(8,128)} %copy-done.3) | copy-start | bytes 3145732
  2325.8 404.4 %copy-start.6 = (bf16[128,8192]{1,0:T(8,128)(2,1)S(1)}, bf16[128,8192]{1,0:T(8,128)(2,1)}, u32[]{:S(2)}) copy-start(bf16[128,8192]{1,0:T(8,128)(2,1)} %get-tuple-element.93) | copy-start | bytes 6291460
  2730.2 294.8 %copy-start.45 = (f32[2,32]{1,0:T(2,128)S(1)}, f32[2,32]{1,0:T(2,128)}, u32[]{:S(2)}) copy-start(f32[2,32]{1,0:T(2,128)} %param.25) | copy-start | bytes 772
  2730.2 294.8 %copy-start.46 = (f32[2,32]{1,0:T(2,128)S(1)}, f32[2,32]{1,0:T(2,128)}, u32[]{:S(2)}) copy-start(f32[2,32]{1,0:T(2,128)} %param.30) | copy-start | bytes 772
  2730.2 294.8 %copy-start.47 = (f32[2,32]{1,0:T(2,128)S(1)}, f32[2,32]{1,0:T(2,128)}, u32[]{:S(2)}) copy-start(f32[2,32]{1,0:T(2,128)} %param.35) | copy-start | bytes 772
  3116.8 4.2 copy-start.12
  (35 other events, 62.6 us)
Sparse Core Ops, SparseCore 0:
  10.3 118.9 all-gather.5
  131.6 110.5 all-gather.7
  244.4 392.9 all-gather.9
  639.6 189.1 all-gather.11
  899.1 293.9 reduce-scatter.10
  1195.4 323.5 reduce-scatter.8
  1521.3 397.4 reduce-scatter.14
  1921.2 402.1 reduce-scatter.12
  2325.9 402.1 reduce-scatter.16
  2730.8 286.9 reduce-scatter.18
  3021.3 81.0 all-reduce.2
where the time goes:
time: 3140 us; the launch traced here: 3130 us
  waiting for transfers between devices  2740 us (87%)
  matrix products  225 us (7%)
  blocking collectives  79.5 us (3%)
  other arithmetic  38.3 us (1%)
    reduce_scatter x3, waiting for transfers between devices, local(): lax.psum_scatter(unit_rows(column_part, token_part, jnp.int32(0), lax.axi...  1200 us
    all_gather x1, waiting for transfers between devices, local(): lax.all_gather(gate_up.astype(jnp.bfloat16), 'shard', axis=2, tiled=True)  389 us
    reduce_scatter x1, waiting for transfers between devices, local(): lax.psum_scatter(term_in, 'shard', scatter_dimension=0, tiled=True)  324 us
    unnamed x12, waiting for transfers between devices  274 us
    reduce_scatter x1, waiting for transfers between devices, local(): lax.psum_scatter(term_out, 'shard', scatter_dimension=0, tiled=True)  169 us
    all_gather x1, waiting for transfers between devices, local(): lax.all_gather(down_weight.astype(jnp.bfloat16), 'shard', axis=0, tiled=T...  160 us
    all_gather x1, waiting for transfers between devices, local(): lax.all_gather(project_out.astype(jnp.bfloat16), 'shard', axis=0, tiled=T...  103 us
    dot_general x5, matrix products, left_dot(): lax.dot_general(left_rows, right_rows, (((0,), (0,)), ((), ())), preferre...  90.1 us
  transfers between devices with their start and end apart: 11, of which 11 were waited for; matrix products, arithmetic and copies ran while one was open for 6% of the time, Pallas kernels for 0%

commit v1 on v0

v1 whole, which is shorter than its diff:
```python
import jax
import jax.numpy as jnp
from jax import lax
from jax.sharding import PartitionSpec as P

HEADS = 32
KV_HEADS = 8
HEAD_DIM = 64
STEP = 10
GROUP = HEADS // KV_HEADS
EVERY = ("rep", "shard")

eps_norm = 1e-05
rope_base = 500000.0
beta_one = 0.9
beta_two = 0.95
adam_eps = 1e-08
rate_matrix = 0.1
rate_gain = 1.0
decay_matrix = 0.1

low_type = jnp.bfloat16
f32 = jnp.float32


def pairs_of(move):
    pairs = []
    for device in range(128):
        c, y, x = device % 2, device // 2 % 4, device // 8 % 2
        z, rep = device // 16 % 4, device // 64
        rep, z, x, y, c = move(rep, z, x, y, c)
        pairs.append((device, rep * 64 + ((z * 2 + x) * 4 + y) * 2 + c))
    return pairs


def x_moved(rep, x, by):
    at = (rep * 2 + x + by) % 4
    return at // 2, at % 2


def go_y(by):
    return pairs_of(lambda rep, z, x, y, c: (rep, z, x, (y + by) % 4, c))


def go_z(by):
    return pairs_of(lambda rep, z, x, y, c: (rep, (z + by) % 4, x, y, c))


def go_x(by):
    def move(rep, z, x, y, c):
        rep, x = x_moved(rep, x, by)
        return rep, z, x, y, c

    return pairs_of(move)


go_core = pairs_of(lambda rep, z, x, y, c: (rep, z, x, y, 1 - c))
go_rep = pairs_of(lambda rep, z, x, y, c: (1 - rep, z, x, y, c))
go_turn = pairs_of(lambda rep, z, x, y, c: (rep, y, c, z, x))


def send(value, pairs):
    return lax.ppermute(value, EVERY, pairs)


def ring_gather(own, step):
    half = own.shape[0] // 2
    left = send(own, step(1))
    right = send(own, step(-1))
    across = jnp.concatenate([send(left[:half], step(1)), send(right[half:], step(-1))])
    return own, left, right, across


def ring_reduce(own, left, right, across, step):
    half = own.shape[0] // 2
    to_right = send(across[:half], step(1))
    to_left = send(across[half:], step(-1))
    right = jnp.concatenate([added(right[:half], to_right), right[half:]])
    left = jnp.concatenate([left[:half], added(left[half:], to_left)])
    got_left = send(right, step(1))
    got_right = send(left, step(-1))
    return own.astype(f32) + got_left.astype(f32) + got_right.astype(f32)


def added(one, two):
    return (one.astype(f32) + two.astype(f32)).astype(low_type)


token_groups = [[f * 8 + t for t in range(8)] for f in range(8)]
y_groups = [[f * 8 + y * 2 + c for y in range(4)] for f in range(8) for c in range(2)]
z_groups = [[z * 16 + x * 8 + t for z in range(4)] for x in range(2) for t in range(8)]


def swap(parts, groups):
    return lax.all_to_all(parts, "shard", 0, 0, axis_index_groups=groups, tiled=True)


def gather(own, groups):
    return swap(jnp.broadcast_to(own[None], (len(groups[0]),) + own.shape), groups)


def gather_tokens(own):
    mine = gather(own, y_groups)
    return mine, jnp.concatenate([mine, send(mine, go_core)])


def reduce_tokens(parts):
    half = parts.shape[0] // 2
    mine = added(parts[:half], send(parts[half:], go_core))
    return swap(mine.reshape((4, -1) + mine.shape[1:]), y_groups).astype(f32).sum(axis=0)


def mate_along_x(own):
    half = own.shape[0] // 2
    return jnp.concatenate([send(own[:half], go_x(1)), send(own[half:], go_x(-1))])


def gather_weights(own):
    own, left, right, across = ring_gather(own, go_z)
    others = [send(left, go_x(1)), send(right, go_x(-1))]
    return [own, left, right, across, mate_along_x(own)] + others + [mate_along_x(across)]


def reduce_weights(blocks):
    across = added(blocks[3], mate_along_x(blocks[7]))
    left = added(blocks[1], send(blocks[5], go_x(-1)))
    right = added(blocks[2], send(blocks[6], go_x(1)))
    own = added(blocks[0], mate_along_x(blocks[4]))
    return ring_reduce(own, left, right, across, go_z)


def sum_replicas(part):
    return part.astype(f32) + send(part.astype(low_type), go_rep).astype(f32)


def gather_small(own, x):
    column = gather(own, z_groups)
    other = mate_along_x(column)
    both = jnp.stack([jnp.where(x == 0, column, other), jnp.where(x == 0, other, column)], axis=1)
    return both.reshape((8,) + own.shape)


def reduce_small(parts, x):
    column = swap(parts.reshape((4, 2) + parts.shape[1:]), z_groups)
    column = column.astype(f32).sum(axis=0).astype(low_type)
    mine = lax.dynamic_index_in_dim(column, x, 0, keepdims=False)
    mates = lax.dynamic_index_in_dim(column, 1 - x, 0, keepdims=False)
    total = mine.astype(f32) + send(mates, go_x(1)).astype(f32)
    return total + send(mates, go_x(-1)).astype(f32) + send(mine, go_rep).astype(f32)


def after(value, *earlier):
    return lax.optimization_barrier((value,) + earlier)[0]


def positions_of(segments):
    seq_len = segments.shape[-1]
    token_index = jnp.arange(seq_len, dtype=jnp.int32)
    changes = jnp.concatenate(
        [
            jnp.ones_like(segments[..., :1]),
            (segments[..., 1:] != segments[..., :-1]).astype(jnp.int32),
        ],
        axis=-1,
    )
    starts = jnp.where(changes > 0, token_index, 0)
    return token_index - lax.cummax(starts, axis=segments.ndim - 1)


def rotate(vectors, cosine, sine):
    half_dim = vectors.shape[-1] // 2
    first_half = vectors[..., :half_dim]
    second_half = vectors[..., half_dim:]
    return jnp.concatenate(
        [
            first_half * cosine - second_half * sine,
            second_half * cosine + first_half * sine,
        ],
        axis=-1,
    )


def normalize(values):
    inverse = lax.rsqrt(jnp.mean(values * values, axis=-1, keepdims=True) + eps_norm)
    return (values * inverse, inverse)


def norm_back(grad_unit, unit_rows, inverse):
    return inverse * (
        grad_unit - unit_rows * jnp.mean(grad_unit * unit_rows, axis=-1, keepdims=True)
    )


def adam_update(master, gradient, moment_old, square_old, step_rate, decay_rate):
    moment_new = beta_one * moment_old + (1.0 - beta_one) * gradient
    square_new = beta_two * square_old + (1.0 - beta_two) * gradient * gradient
    moment_hat = moment_new / (1.0 - beta_one**STEP)
    square_hat = square_new / (1.0 - beta_two**STEP)
    updated = master - step_rate * (
        moment_hat / (jnp.sqrt(square_hat) + adam_eps) + decay_rate * master
    )
    return (updated, moment_new, square_new)


def dot(left_rows, right_rows):
    return jnp.dot(left_rows, right_rows, preferred_element_type=f32)


def left_dot(left_rows, right_rows):
    return lax.dot_general(
        left_rows, right_rows, (((0,), (0,)), ((), ())), preferred_element_type=f32
    )


def right_dot(left_rows, right_rows):
    return lax.dot_general(
        left_rows, right_rows, (((1,), (1,)), ((), ())), preferred_element_type=f32
    )


def masked_scores(queries, key_rows, allowed):
    scores = jnp.einsum("sagd,scd->sgac", queries, key_rows, preferred_element_type=f32)
    return jnp.where(allowed[:, None], scores * HEAD_DIM ** (-0.5), -1e30)


def local(
    tokens,
    cotangent,
    segments,
    project_in,
    project_out,
    gate_up,
    down_weight,
    norm_gains,
    first_in,
    first_out,
    first_gate,
    first_down,
    first_gains,
    second_in,
    second_out,
    second_gate,
    second_down,
    second_gains,
):
    place = lax.axis_index("shard")
    c, x = place % 2, place // 8 % 2
    seq_len, width = tokens.shape
    inputs = tokens.astype(f32)
    grad_out = cotangent.astype(f32)

    gains_low = norm_gains.astype(low_type)
    gain_rows = gains_low[0].astype(f32)[:, None]
    low_in = project_in.astype(low_type).astype(f32)
    folded = (low_in * gain_rows).astype(low_type)
    query_width, kv_width = HEADS * HEAD_DIM, KV_HEADS * HEAD_DIM
    own_rows = folded.shape[0]
    by_group = jnp.concatenate(
        [
            folded[:, :query_width].reshape(own_rows, KV_HEADS, GROUP * HEAD_DIM),
            folded[:, query_width : query_width + kv_width].reshape(own_rows, KV_HEADS, HEAD_DIM),
            folded[:, query_width + kv_width :].reshape(own_rows, KV_HEADS, HEAD_DIM),
        ],
        axis=2,
    )
    group_width = by_group.shape[2]
    by_source = swap(by_group.transpose(1, 0, 2), token_groups)
    head_in = gather_small(by_source.reshape(8 * own_rows, group_width), x)
    head_in = head_in.reshape(-1, group_width)

    own_gu = jnp.concatenate([gate_up[0].astype(low_type).T, gate_up[1].astype(low_type).T])
    units_own = down_weight.shape[0]
    blocks = gather_weights(jnp.concatenate([own_gu, down_weight.astype(low_type)]))

    seg_all = gather(segments, token_groups).reshape(4, 2, seq_len)
    seg_all = jnp.concatenate(
        [lax.dynamic_index_in_dim(seg_all, core, 1, keepdims=False) for core in (c, 1 - c)]
    )
    position = positions_of(seg_all)
    token_index = jnp.arange(seq_len, dtype=jnp.int32)
    allowed = (seg_all[:, :, None] == seg_all[:, None, :]) & (
        token_index[None, :, None] >= token_index[None, None, :]
    )
    frequency = rope_base ** (-jnp.arange(HEAD_DIM // 2, dtype=f32) * 2.0 / HEAD_DIM)
    angles = position.astype(f32)[..., None] * frequency
    cosine, sine = jnp.cos(angles)[:, :, None], jnp.sin(angles)[:, :, None]

    unit_one, inverse_one = normalize(inputs)
    some_units, units_one = gather_tokens(after(unit_one.astype(low_type), head_in))
    units_one = after(units_one.reshape(-1, width), blocks[1], blocks[2])

    gain_tile = jnp.pad(gains_low[1:], ((0, 15), (0, width - own_rows)))
    out_tile = jnp.concatenate([project_out.astype(low_type), gain_tile])
    out_tiles = gather_small(after(send(out_tile, go_turn), some_units), x)
    head_out = out_tiles[:, :own_rows].reshape(-1, width)
    gain_two = gather(out_tiles[:, own_rows, :own_rows].reshape(1, -1), token_groups)
    gain_two = gain_two.reshape(width).astype(f32)
    cots = gather_tokens(after(cotangent, out_tiles))[1].reshape(-1, width)
    mixed = dot(units_one, head_in).reshape(8, seq_len, group_width)
    q_width = GROUP * HEAD_DIM
    queries = rotate(mixed[..., :q_width].reshape(8, seq_len, GROUP, HEAD_DIM), cosine, sine)
    queries = queries.astype(low_type)
    key_rows = rotate(mixed[..., None, q_width : q_width + HEAD_DIM], cosine, sine)[:, :, 0]
    key_rows = key_rows.astype(low_type)
    values = mixed[..., q_width + HEAD_DIM :].astype(low_type)
    soft_probs = jax.nn.softmax(masked_scores(queries, key_rows, allowed), axis=-1)
    low_probs = soft_probs.astype(low_type)
    attended = jnp.einsum("sgac,scd->sagd", low_probs, values, preferred_element_type=f32)
    attended = attended.reshape(8 * seq_len, q_width).astype(low_type)
    hidden = inputs + reduce_tokens(dot(attended, head_out).astype(low_type))

    hidden = after(hidden, *blocks[3:7])
    weight_gu = jnp.concatenate(
        [block[:units_own] for block in blocks]
        + [block[units_own : 2 * units_own] for block in blocks]
    )
    weight_down = jnp.concatenate([block[2 * units_own :] for block in blocks])
    unit_two, inverse_two = normalize(hidden)
    normed = gather_tokens((unit_two * gain_two).astype(low_type))[1].reshape(-1, width)
    rows = 8 * seq_len
    units = 8 * units_own
    pre = right_dot(normed, weight_gu)
    gate_pre, up_pre = pre[:, :units], pre[:, units:]
    grad_act = right_dot(cots, weight_down)
    sigmoid_gate = jax.nn.sigmoid(gate_pre)
    activated = (gate_pre * sigmoid_gate * up_pre).astype(low_type)
    grad_gate = grad_act * up_pre * sigmoid_gate * (1.0 + gate_pre * (1.0 - sigmoid_gate))
    grad_up = grad_act * gate_pre * sigmoid_gate
    grad_gu = jnp.concatenate([grad_gate.astype(low_type), grad_up.astype(low_type)], axis=1)
    grad_normed_two = reduce_tokens(dot(grad_gu, weight_gu).astype(low_type))
    term_gu = left_dot(grad_gu, normed).astype(low_type).reshape(2, 8, units_own, width)
    term_down = left_dot(activated, cots).astype(low_type).reshape(8, units_own, width)
    terms = [jnp.concatenate([term_gu[0, i], term_gu[1, i], term_down[i]]) for i in range(8)]
    sum_ffn = sum_replicas(reduce_weights(terms))
    sum_gate = jnp.stack([sum_ffn[:units_own].T, sum_ffn[units_own : 2 * units_own].T])
    sum_down = sum_ffn[2 * units_own :]
    layer_out = hidden + reduce_tokens(dot(activated, weight_down).astype(low_type))

    gain_terms = jnp.sum(grad_normed_two * unit_two, axis=0).astype(low_type).reshape(8, -1)
    gain_terms = swap(gain_terms, token_groups).astype(f32).sum(axis=0).astype(low_type)
    grad_hidden = grad_out + norm_back(grad_normed_two * gain_two, unit_two, inverse_two)

    branch = gather_tokens(grad_hidden.astype(low_type))[1].reshape(-1, width)
    term_out = left_dot(attended, branch).astype(low_type)
    grad_attended = right_dot(branch, head_out).astype(low_type)
    grad_attended = grad_attended.reshape(8, seq_len, GROUP, HEAD_DIM)
    grad_values = jnp.einsum(
        "sgac,sagd->scd", low_probs, grad_attended, preferred_element_type=f32
    )
    grad_probs = jnp.einsum("sagd,scd->sgac", grad_attended, values, preferred_element_type=f32)
    row_inner = jnp.sum(soft_probs * grad_probs, axis=-1, keepdims=True)
    grad_scores = (soft_probs * (grad_probs - row_inner) * HEAD_DIM ** (-0.5)).astype(low_type)
    grad_queries = jnp.einsum("sgac,scd->sagd", grad_scores, key_rows, preferred_element_type=f32)
    grad_keys = jnp.einsum("sgac,sagd->scd", grad_scores, queries, preferred_element_type=f32)
    grad_queries = rotate(grad_queries, cosine, -sine).reshape(8, seq_len, q_width)
    grad_keys = rotate(grad_keys[:, :, None], cosine, -sine)[:, :, 0]
    grad_mixed = jnp.concatenate([grad_queries, grad_keys, grad_values], axis=-1)
    grad_mixed = grad_mixed.reshape(rows, group_width).astype(low_type)
    grad_unit_one = reduce_tokens(right_dot(grad_mixed, head_in).astype(low_type))
    input_grad = grad_hidden + norm_back(grad_unit_one, unit_one, inverse_one)
    term_in = left_dot(units_one, grad_mixed).astype(low_type)

    gain_tiles = jnp.pad(
        gain_terms.reshape(8, 1, own_rows), ((0, 0), (0, 15), (0, width - own_rows))
    )
    out_tiles = jnp.concatenate([term_out.reshape(8, own_rows, width), gain_tiles], axis=1)
    sum_tile = send(reduce_small(out_tiles, x).astype(low_type), go_turn).astype(f32)
    sum_out, sum_gain_two = sum_tile[:own_rows], sum_tile[own_rows, :own_rows]
    chunk = reduce_small(term_in.reshape(8, 8 * own_rows, group_width), x).astype(low_type)
    groups = swap(chunk.reshape(8, own_rows, group_width), token_groups).transpose(1, 0, 2)
    sum_unit = jnp.concatenate(
        [
            groups[:, :, :q_width].reshape(own_rows, query_width),
            groups[:, :, q_width : q_width + HEAD_DIM].reshape(own_rows, kv_width),
            groups[:, :, q_width + HEAD_DIM :].reshape(own_rows, kv_width),
        ],
        axis=1,
    ).astype(f32)
    sum_in = sum_unit * gain_rows
    sum_gains = jnp.stack([jnp.sum(sum_unit * low_in, axis=1), sum_gain_two])

    new_in, moment_in, square_in = adam_update(
        project_in, sum_in, first_in, second_in, rate_matrix, decay_matrix
    )
    new_out, moment_out, square_out = adam_update(
        project_out, sum_out, first_out, second_out, rate_matrix, decay_matrix
    )
    new_gate, moment_gate, square_gate = adam_update(
        gate_up, sum_gate, first_gate, second_gate, rate_matrix, decay_matrix
    )
    new_down, moment_down, square_down = adam_update(
        down_weight, sum_down, first_down, second_down, rate_matrix, decay_matrix
    )
    new_gains, moment_gains, square_gains = adam_update(
        norm_gains, sum_gains, first_gains, second_gains, rate_gain, 0.0
    )
    return (
        layer_out,
        input_grad,
        new_in,
        new_out,
        new_gate,
        new_down,
        new_gains,
        moment_in,
        moment_out,
        moment_gate,
        moment_down,
        moment_gains,
        square_in,
        square_out,
        square_gate,
        square_down,
        square_gains,
    )


def solution(mesh):
    tokens_split = P(EVERY, None)
    weights = (P("shard", None), P("shard", None), P(None, None, "shard"), P("shard", None), P(None, "shard"))
    in_specs = (tokens_split,) * 3 + weights * 3
    out_specs = (tokens_split,) * 2 + weights * 3
    return jax.shard_map(local, mesh=mesh, in_specs=in_specs, out_specs=out_specs, check_vma=False)
```

time: 3140 us -> 659 us (0.21)
  waiting for transfers between devices: 2740 us -> 190 us
  starting transfers between devices: 0.46 us -> 144 us
  matrix products: 225 us -> 93.7 us
  blocking collectives: 79.5 us -> 0 us
  local copies, waits for them, and re-layouts: 30.9 us -> 108 us
  other arithmetic: 38.3 us -> 111 us
    reduce_scatter x5 -> x0, waiting for transfers between devices: 1700 us -> none  [the longest x3 1200 us: local(): lax.psum_scatter(unit_rows(column_part, token_part, jnp.int32(0), lax.axi...]
    all_gather x4 -> x0, waiting for transfers between devices: 693 us -> none  [the longest x1 389 us: local(): lax.all_gather(gate_up.astype(jnp.bfloat16), 'shard', axis=2, tiled=True)]
    unnamed x12 -> x0, waiting for transfers between devices: 274 us -> none
    ppermute x0 -> x41, waiting for transfers between devices: none -> 99.6 us  [send(): return lax.ppermute(value, EVERY, pairs)]
    all_to_all x0 -> x17, starting transfers between devices: none -> 93 us  [swap(): lax.all_to_all(parts, 'shard', 0, 0, axis_index_groups=groups, tiled=True)]
    all_to_all x0 -> x17, waiting for transfers between devices: none -> 90.3 us  [swap(): lax.all_to_all(parts, 'shard', 0, 0, axis_index_groups=groups, tiled=True)]
    psum x1 -> x0, waiting for transfers between devices: 76.8 us -> none  [local(): lax.psum(own_in.astype(jnp.bfloat16), 'rep').astype(jnp.float32)]
    all_gather x1 -> x0, blocking collectives: 73.1 us -> none  [local(): lax.all_gather(norm_gains.astype(jnp.bfloat16), 'shard', axis=1, tiled=True)]
  transfers between devices with their start and end apart: 11 -> 58, of which waited for: 11 -> 19; matrix products, arithmetic and copies ran while one was open for 6% -> 38% of each run, Pallas kernels for 0% -> 0%
where the time goes in v1:
time: 659 us; the launch traced here: 649 us
  waiting for transfers between devices  190 us (29%)
  starting transfers between devices  144 us (22%)
  other arithmetic  111 us (17%)
  local copies, waits for them, and re-layouts  108 us (16%)
  matrix products  93.7 us (14%)
    ppermute x41, waiting for transfers between devices, send(): return lax.ppermute(value, EVERY, pairs)  99.6 us
    all_to_all x17, starting transfers between devices, swap(): lax.all_to_all(parts, 'shard', 0, 0, axis_index_groups=groups, tiled=True)  93 us
    all_to_all x17, waiting for transfers between devices, swap(): lax.all_to_all(parts, 'shard', 0, 0, axis_index_groups=groups, tiled=True)  90.3 us
    unnamed x173, local copies, waits for them, and re-layouts  62.6 us
    ppermute x41, starting transfers between devices, send(): return lax.ppermute(value, EVERY, pairs)  50.8 us
    dot_general x4, matrix products, right_dot(): lax.dot_general(left_rows, right_rows, (((1,), (1,)), ((), ())), preferre...  28.9 us
    convert_element_type x9, other arithmetic, added(): return (one.astype(f32) + two.astype(f32)).astype(low_type)  25.8 us
    dot_general x4, matrix products, dot(): return jnp.dot(left_rows, right_rows, preferred_element_type=f32)  23.6 us
  transfers between devices with their start and end apart: 58, of which 19 were waited for; matrix products, arithmetic and copies ran while one was open for 38% of the time, Pallas kernels for 0%

profile of v1, /device:TPU:24, one launch (start us, length us, event | category | flops | bytes accessed | tf_op | source)
XLA Modules:
  0.0 648.8 jit_solution(9499558686349589677)
XLA Ops:
  26.4 8.0 %all-to-all-done.1 = bf16[4,256,384]{2,1,0:T(8,128)(2,1)S(1)} async-done(((bf16[4,256,384]{2,1,0:T(8,128)(2,1)}), bf16[4,256,384]{2,1,0:T(8,128)(2,1)S(1)}, u32[]{:S(2)}, u32[]{:S(2)}) %all-to-all-start.1) | async-done | bytes 786464 | tf_op jit(solution)/shard_map/all_to_all | solution.py:95
  44.6 8.2 %collective-permute-done = bf16[2,256,384]{2,1,0:T(8,128)(2,1)S(1)} collective-permute-done((bf16[2,256,384]{2,1,0:T(8,128)(2,1)S(1)}, bf16[2,256,384]{2,1,0:T(8,128)(2,1)S(1)}, u32[]{:S(2)}, u32[]{:S(2)}) %collective-permute-start) | collective-permute-done | bytes 393248 | tf_op jit(solution)/shard_map/ppermute | solution.py:63
  69.5 24.1 %collective-permute-done.5 = bf16[48,2048]{1,0:T(8,128)(2,1)S(1)} collective-permute-done((bf16[48,2048]{1,0:T(8,128)(2,1)S(1)}, bf16[48,2048]{1,0:T(8,128)(2,1)S(1)}, u32[]{:S(2)}, u32[]{:S(2)}) %collective-permute-start.5) | collective-permute-done | bytes 196640 | tf_op jit(solution)/shard_map/ppermute | solution.py:63
  100.2 7.3 %all-to-all-done.4 = bf16[4,48,2048]{2,1,0:T(8,128)(2,1)S(1)} async-done(((bf16[4,48,2048]{2,1,0:T(8,128)(2,1)}), bf16[4,48,2048]{2,1,0:T(8,128)(2,1)S(1)}, u32[]{:S(2)}, u32[]{:S(2)}) %all-to-all-start.4) | async-done | bytes 786464 | tf_op jit(solution)/shard_map/all_to_all | solution.py:95
  168.6 6.4 all-to-all-start.6
  191.1 18.1 %all-to-all-done.5 = bf16[4,128,2048]{2,1,0:T(8,128)(2,1)} async-done(((bf16[4,128,2048]{2,1,0:T(8,128)(2,1)}), bf16[4,128,2048]{2,1,0:T(8,128)(2,1)}, u32[]{:S(2)}, u32[]{:S(2)}) %all-to-all-start.5) | async-done | bytes 2097184 | tf_op jit(solution)/shard_map/all_to_all | solution.py:95
  210.9 6.5 %all-to-all-start.9 = ((bf16[4,128,2048]{2,1,0:T(8,128)(2,1)}), bf16[4,128,2048]{2,1,0:T(8,128)(2,1)}, u32[]{:S(2)}, u32[]{:S(2)}) async-start(bf16[4,128,2048]{2,1,0:T(8,128)(2,1)} %broadcast_in_dim.57), calls=%async_computation.9 | async-start | bytes 4194304 | tf_op jit(solution)/shard_map/all_to_all | solution.py:95
  220.0 21.3 %all-to-all-done.9 = bf16[4,128,2048]{2,1,0:T(8,128)(2,1)} async-done(((bf16[4,128,2048]{2,1,0:T(8,128)(2,1)}), bf16[4,128,2048]{2,1,0:T(8,128)(2,1)}, u32[]{:S(2)}, u32[]{:S(2)}) %all-to-all-start.9) | async-done | bytes 2097184 | tf_op jit(solution)/shard_map/all_to_all | solution.py:95
  242.8 5.7 all-to-all-start.7
  257.2 14.1 %all-to-all-done.7 = bf16[4,128,2048]{2,1,0:T(8,128)(2,1)S(1)} async-done(((bf16[4,128,2048]{2,1,0:T(8,128)(2,1)}), bf16[4,128,2048]{2,1,0:T(8,128)(2,1)S(1)}, u32[]{:S(2)}, u32[]{:S(2)}) %all-to-all-start.7) | async-done | bytes 2097184 | tf_op jit(solution)/shard_map/all_to_all | solution.py:95
  283.6 14.8 %fusion.91 = f32[1024,2048]{1,0:T(8,128)} fusion(bf16[1024,2048]{1,0:T(8,128)(2,1)S(1)} %bitcast.231, bf16[2048,2048]{1,0:T(8,128)(2,1)} %get-tuple-element.200), kind=kOutput, calls=%fused_computation.264 | convolution fusion | flops 8589934592 | bytes 20971520 | tf_op jit(solution)/shard_map/dot_general | solution.py:216
  298.4 9.7 %multiply_convert_fusion.1 = (bf16[1024,1024]{1,0:T(8,128)(2,1)S(1)}, bf16[1024,1024]{1,0:T(8,128)(2,1)}, bf16[1024,1024]{1,0:T(8,128)(2,1)S(1)}) fusion(f32[1024,2048]{1,0:T(8,128)} %fusion.91, bf16[1024,2048]{1,0:T(8,128)(2,1)S(1)} %bitcast.229, bf16[1024,2048]{1,0:T(8,128)(2,1)S(1)} %copy-done.55), kind=kOutput, calls=%fused_computation.13 | convolution fusion | flops 4311744512 | bytes 23068672 | tf_op jit(solution)/shard_map/dot_general | solution.py:216
  308.1 12.7 %convolution_convert_fusion.2 = bf16[1024,2048]{1,0:T(8,128)(2,1)S(1)} fusion(bf16[2048,2048]{1,0:T(8,128)(2,1)} %get-tuple-element.200, bf16[1024,1024]{1,0:T(8,128)(2,1)} %get-tuple-element.149, bf16[1024,1024]{1,0:T(8,128)(2,1)S(1)} %get-tuple-element.148), kind=kOutput, calls=%fused_computation.21 | convolution fusion | flops 8600420352 | bytes 16777216 | tf_op jit(solution)/shard_map/dot_general | solution.py:206
  320.7 11.9 %convolution_convert_fusion = bf16[2048,2048]{1,0:T(8,128)(2,1)S(1)} fusion(bf16[1024,2048]{1,0:T(8,128)(2,1)} %bitcast.232, bf16[1024,1024]{1,0:T(8,128)(2,1)} %get-tuple-element.149, bf16[1024,1024]{1,0:T(8,128)(2,1)S(1)} %get-tuple-element.148), kind=kOutput, calls=%fused_computation.2 | convolution fusion | flops 8602517504 | bytes 16777216 | tf_op jit(solution)/shard_map/dot_general | solution.py:210
  350.3 6.7 %all-to-all-start.10 = ((bf16[4,128,2048]{2,1,0:T(8,128)(2,1)}), bf16[4,128,2048]{2,1,0:T(8,128)(2,1)}, u32[]{:S(2)}, u32[]{:S(2)}) async-start(bf16[4,128,2048]{2,1,0:T(8,128)(2,1)} %bitcast.38), calls=%async_computation.10 | async-start | bytes 4194304 | tf_op jit(solution)/shard_map/all_to_all | solution.py:95
  357.1 7.3 %convolution_convert_fusion.5 = bf16[1024,2048]{1,0:T(8,128)(2,1)S(1)} fusion(bf16[1024,1024]{1,0:T(8,128)(2,1)} %copy-done.66, bf16[1024,2048]{1,0:T(8,128)(2,1)} %get-tuple-element.199), kind=kOutput, calls=%fused_computation.24 | convolution fusion | flops 4297064448 | bytes 10485760 | tf_op jit(solution)/shard_map/dot_general | solution.py:206
  374.4 22.7 %collective-permute-done.37 = bf16[384,2048]{1,0:T(8,128)(2,1)} collective-permute-done((bf16[384,2048]{1,0:T(8,128)(2,1)}, bf16[384,2048]{1,0:T(8,128)(2,1)}, u32[]{:S(2)}, u32[]{:S(2)}) %collective-permute-start.37) | collective-permute-done | bytes 1572896 | tf_op jit(solution)/shard_map/ppermute | solution.py:63
  404.6 6.5 all-to-all-start.11
  420.9 14.2 %all-to-all-done.11 = bf16[4,128,2048]{2,1,0:T(8,128)(2,1)} async-done(((bf16[4,128,2048]{2,1,0:T(8,128)(2,1)}), bf16[4,128,2048]{2,1,0:T(8,128)(2,1)}, u32[]{:S(2)}, u32[]{:S(2)}) %all-to-all-start.11) | async-done | bytes 2097184 | tf_op jit(solution)/shard_map/all_to_all | solution.py:95
  439.5 6.5 %all-to-all-start.8 = ((bf16[4,128,2048]{2,1,0:T(8,128)(2,1)}), bf16[4,128,2048]{2,1,0:T(8,128)(2,1)}, u32[]{:S(2)}, u32[]{:S(2)}) async-start(bf16[4,128,2048]{2,1,0:T(8,128)(2,1)} %bitcast.220), calls=%async_computation.8 | async-start | bytes 4194304 | tf_op jit(solution)/shard_map/all_to_all | solution.py:95
  456.9 11.8 %collective-permute-done.31 = bf16[192,2048]{1,0:T(8,128)(2,1)} collective-permute-done((bf16[192,2048]{1,0:T(8,128)(2,1)}, bf16[192,2048]{1,0:T(8,128)(2,1)}, u32[]{:S(2)}, u32[]{:S(2)}) %collective-permute-start.31) | collective-permute-done | bytes 786464 | tf_op jit(solution)/shard_map/ppermute | solution.py:63
  540.1 6.8 %all-to-all-done.13 = bf16[4,2,256,384]{3,2,1,0:T(8,128)(2,1)} async-done(((bf16[4,2,256,384]{3,2,1,0:T(8,128)(2,1)}), bf16[4,2,256,384]{3,2,1,0:T(8,128)(2,1)}, u32[]{:S(2)}, u32[]{:S(2)}) %all-to-all-start.13) | async-done | bytes 1572896 | tf_op jit(solution)/shard_map/all_to_all | solution.py:95
  600.1 6.5 all-to-all-start.12
  617.4 23.3 %collective-permute-done.29 = bf16[48,2048]{1,0:T(8,128)(2,1)S(1)} collective-permute-done((bf16[48,2048]{1,0:T(8,128)(2,1)}, bf16[48,2048]{1,0:T(8,128)(2,1)S(1)}, u32[]{:S(2)}, u32[]{:S(2)}) %collective-permute-start.29) | collective-permute-done | bytes 196640 | tf_op jit(solution)/shard_map/ppermute | solution.py:63
  (424 shorter events, 365.7 us)
Async XLA Ops:
  22.9 90.0 %collective-permute-start.3 = (bf16[384,2048]{1,0:T(8,128)(2,1)}, bf16[384,2048]{1,0:T(8,128)(2,1)}, u32[]{:S(2)}, u32[]{:S(2)}) collective-permute-start(bf16[384,2048]{1,0:T(8,128)(2,1)} %pad_maximum_fusion.9), channel_id=1, source_target_pairs={{0,16},{1,17},{2,18},{3,19},{4,20},{5,21},{6,22},{7,23},{8,24},{9,... | collective-permute-start | bytes 4718600 | tf_op jit(solution)/shard_map/ppermute | solution.py:63
  25.0 91.2 %collective-permute-start.4 = (bf16[384,2048]{1,0:T(8,128)(2,1)}, bf16[384,2048]{1,0:T(8,128)(2,1)}, u32[]{:S(2)}, u32[]{:S(2)}) collective-permute-start(bf16[384,2048]{1,0:T(8,128)(2,1)} %pad_maximum_fusion.9), channel_id=1, source_target_pairs={{0,48},{1,49},{2,50},{3,51},{4,52},{5,53},{6,54},{7,55},{8,56},{9,... | collective-permute-start | bytes 4718600 | tf_op jit(solution)/shard_map/ppermute | solution.py:63
  56.1 37.5 %all-to-all-start.2 = ((bf16[4,128,2048]{2,1,0:T(8,128)(2,1)}), bf16[4,128,2048]{2,1,0:T(8,128)(2,1)}, u32[]{:S(2)}, u32[]{:S(2)}) async-start(bf16[4,128,2048]{2,1,0:T(8,128)(2,1)} %broadcast_in_dim.42), calls=%async_computation.2 | async-start | bytes 4194304 | tf_op jit(solution)/shard_map/all_to_all | solution.py:95
  62.2 45.3 %collective-permute-start.11 = (bf16[192,2048]{1,0:T(8,128)(2,1)}, bf16[192,2048]{1,0:T(8,128)(2,1)}, u32[]{:S(2)}, u32[]{:S(2)}) collective-permute-start(bf16[192,2048]{1,0:T(8,128)(2,1)} %get-tuple-element.211), channel_id=1, source_target_pairs={{0,8},{1,9},{2,10},{3,11},{4,12},{5,13},{6,14},{7,15},{8,64},{9,65... | collective-permute-start | bytes 2359304 | tf_op jit(solution)/shard_map/ppermute | solution.py:63
  63.7 47.6 %collective-permute-start.12 = (bf16[192,2048]{1,0:T(8,128)(2,1)}, bf16[192,2048]{1,0:T(8,128)(2,1)S(1)}, u32[]{:S(2)}, u32[]{:S(2)}) collective-permute-start(bf16[192,2048]{1,0:T(8,128)(2,1)} %get-tuple-element.210), channel_id=1, source_target_pairs={{0,72},{1,73},{2,74},{3,75},{4,76},{5,77},{6,78},{7,79},{8,0},{9,1... | collective-permute-start | bytes 2359304 | tf_op jit(solution)/shard_map/ppermute | solution.py:63
  115.6 39.8 %collective-permute-start.9 = (bf16[192,2048]{1,0:T(8,128)(2,1)}, bf16[192,2048]{1,0:T(8,128)(2,1)}, u32[]{:S(2)}, u32[]{:S(2)}) collective-permute-start(bf16[192,2048]{1,0:T(8,128)(2,1)} %slice.447), channel_id=1, source_target_pairs={{0,16},{1,17},{2,18},{3,19},{4,20},{5,21},{6,22},{7,23},{8,24},{9,... | collective-permute-start | bytes 2359304 | tf_op jit(solution)/shard_map/ppermute | solution.py:63
  118.3 37.2 %collective-permute-start.10 = (bf16[192,2048]{1,0:T(8,128)(2,1)}, bf16[192,2048]{1,0:T(8,128)(2,1)}, u32[]{:S(2)}, u32[]{:S(2)}) collective-permute-start(bf16[192,2048]{1,0:T(8,128)(2,1)} %slice.448), channel_id=1, source_target_pairs={{0,48},{1,49},{2,50},{3,51},{4,52},{5,53},{6,54},{7,55},{8,56},{9,... | collective-permute-start | bytes 2359304 | tf_op jit(solution)/shard_map/ppermute | solution.py:63
  121.4 63.2 %collective-permute-start.13 = (bf16[384,2048]{1,0:T(8,128)(2,1)}, bf16[384,2048]{1,0:T(8,128)(2,1)}, u32[]{:S(2)}, u32[]{:S(2)}) collective-permute-start(bf16[384,2048]{1,0:T(8,128)(2,1)} %collective-permute-done.3), channel_id=1, source_target_pairs={{0,8},{1,9},{2,10},{3,11},{4,12},{5,13},{6,14},{7,15},{8,64},{9,65... | collective-permute-start | bytes 4718600 | tf_op jit(solution)/shard_map/ppermute | solution.py:63
  122.7 63.8 %collective-permute-start.14 = (bf16[384,2048]{1,0:T(8,128)(2,1)}, bf16[384,2048]{1,0:T(8,128)(2,1)}, u32[]{:S(2)}, u32[]{:S(2)}) collective-permute-start(bf16[384,2048]{1,0:T(8,128)(2,1)} %collective-permute-done.4), channel_id=1, source_target_pairs={{0,72},{1,73},{2,74},{3,75},{4,76},{5,77},{6,78},{7,79},{8,0},{9,1... | collective-permute-start | bytes 4718600 | tf_op jit(solution)/shard_map/ppermute | solution.py:63
  155.4 33.0 %collective-permute-start.16 = (bf16[192,2048]{1,0:T(8,128)(2,1)}, bf16[192,2048]{1,0:T(8,128)(2,1)}, u32[]{:S(2)}, u32[]{:S(2)}) collective-permute-start(bf16[192,2048]{1,0:T(8,128)(2,1)} %collective-permute-done.9), channel_id=1, source_target_pairs={{0,8},{1,9},{2,10},{3,11},{4,12},{5,13},{6,14},{7,15},{8,64},{9,65... | collective-permute-start | bytes 2359304 | tf_op jit(solution)/shard_map/ppermute | solution.py:63
  155.4 122.9 %collective-permute-start.17 = (bf16[192,2048]{1,0:T(8,128)(2,1)}, bf16[192,2048]{1,0:T(8,128)(2,1)}, u32[]{:S(2)}, u32[]{:S(2)}) collective-permute-start(bf16[192,2048]{1,0:T(8,128)(2,1)} %collective-permute-done.10), channel_id=1, source_target_pairs={{0,72},{1,73},{2,74},{3,75},{4,76},{5,77},{6,78},{7,79},{8,0},{9,1... | collective-permute-start | bytes 2359304 | tf_op jit(solution)/shard_map/ppermute | solution.py:63
  346.8 50.2 %collective-permute-start.37 = (bf16[384,2048]{1,0:T(8,128)(2,1)}, bf16[384,2048]{1,0:T(8,128)(2,1)}, u32[]{:S(2)}, u32[]{:S(2)}) collective-permute-start(bf16[384,2048]{1,0:T(8,128)(2,1)} %pad_maximum_fusion.14), channel_id=1, source_target_pairs={{0,72},{1,73},{2,74},{3,75},{4,76},{5,77},{6,78},{7,79},{8,0},{9,1... | collective-permute-start | bytes 4718600 | tf_op jit(solution)/shard_map/ppermute | solution.py:63
  350.3 49.9 %all-to-all-start.10 = ((bf16[4,128,2048]{2,1,0:T(8,128)(2,1)}), bf16[4,128,2048]{2,1,0:T(8,128)(2,1)}, u32[]{:S(2)}, u32[]{:S(2)}) async-start(bf16[4,128,2048]{2,1,0:T(8,128)(2,1)} %bitcast.38), calls=%async_computation.10 | async-start | bytes 4194304 | tf_op jit(solution)/shard_map/all_to_all | solution.py:95
  367.0 68.1 %collective-permute-start.18 = (bf16[512,2048]{1,0:T(8,128)(2,1)}, bf16[512,2048]{1,0:T(8,128)(2,1)}, u32[]{:S(2)}, u32[]{:S(2)}) collective-permute-start(bf16[512,2048]{1,0:T(8,128)(2,1)} %slice.473), channel_id=1, source_target_pairs={{0,1},{1,0},{2,3},{3,2},{4,5},{5,4},{6,7},{7,6},{8,9},{9,8},{10,11... | collective-permute-start | bytes 6291464 | tf_op jit(solution)/shard_map/ppermute | solution.py:63
  368.3 46.9 %collective-permute-start.32 = (bf16[384,2048]{1,0:T(8,128)(2,1)}, bf16[384,2048]{1,0:T(8,128)(2,1)}, u32[]{:S(2)}, u32[]{:S(2)}) collective-permute-start(bf16[384,2048]{1,0:T(8,128)(2,1)} %pad_maximum_fusion.12), channel_id=1, source_target_pairs={{0,8},{1,9},{2,10},{3,11},{4,12},{5,13},{6,14},{7,15},{8,64},{9,65... | collective-permute-start | bytes 4718600 | tf_op jit(solution)/shard_map/ppermute | solution.py:63
  372.4 38.7 %collective-permute-start.38 = (bf16[192,2048]{1,0:T(8,128)(2,1)}, bf16[192,2048]{1,0:T(8,128)(2,1)}, u32[]{:S(2)}, u32[]{:S(2)}) collective-permute-start(bf16[192,2048]{1,0:T(8,128)(2,1)} %get-tuple-element.178), channel_id=1, source_target_pairs={{0,48},{1,49},{2,50},{3,51},{4,52},{5,53},{6,54},{7,55},{8,56},{9,... | collective-permute-start | bytes 2359304 | tf_op jit(solution)/shard_map/ppermute | solution.py:63
  373.5 43.8 %collective-permute-start.35 = (bf16[192,2048]{1,0:T(8,128)(2,1)}, bf16[192,2048]{1,0:T(8,128)(2,1)}, u32[]{:S(2)}, u32[]{:S(2)}) collective-permute-start(bf16[192,2048]{1,0:T(8,128)(2,1)} %get-tuple-element.177), channel_id=1, source_target_pairs={{0,16},{1,17},{2,18},{3,19},{4,20},{5,21},{6,22},{7,23},{8,24},{9,... | collective-permute-start | bytes 2359304 | tf_op jit(solution)/shard_map/ppermute | solution.py:63
  414.1 57.3 %collective-permute-start.39 = (bf16[384,2048]{1,0:T(8,128)(2,1)}, bf16[384,2048]{1,0:T(8,128)(2,1)}, u32[]{:S(2)}, u32[]{:S(2)}) collective-permute-start(bf16[384,2048]{1,0:T(8,128)(2,1)} %pad_maximum_fusion.15), channel_id=1, source_target_pairs={{0,48},{1,49},{2,50},{3,51},{4,52},{5,53},{6,54},{7,55},{8,56},{9,... | collective-permute-start | bytes 4718600 | tf_op jit(solution)/shard_map/ppermute | solution.py:63
  420.0 51.4 %collective-permute-start.36 = (bf16[384,2048]{1,0:T(8,128)(2,1)}, bf16[384,2048]{1,0:T(8,128)(2,1)}, u32[]{:S(2)}, u32[]{:S(2)}) collective-permute-start(bf16[384,2048]{1,0:T(8,128)(2,1)} %pad_maximum_fusion.13), channel_id=1, source_target_pairs={{0,16},{1,17},{2,18},{3,19},{4,20},{5,21},{6,22},{7,23},{8,24},{9,... | collective-permute-start | bytes 4718600 | tf_op jit(solution)/shard_map/ppermute | solution.py:63
  435.1 51.7 %collective-permute-start.21 = (bf16[4,128,2048]{2,1,0:T(8,128)(2,1)}, bf16[4,128,2048]{2,1,0:T(8,128)(2,1)}, u32[]{:S(2)}, u32[]{:S(2)}) collective-permute-start(bf16[4,128,2048]{2,1,0:T(8,128)(2,1)} %all-to-all-done.11), channel_id=1, source_target_pairs={{0,1},{1,0},{2,3},{3,2},{4,5},{5,4},{6,7},{7,6},{8,9},{9,8},{10,11... | collective-permute-start | bytes 6291464 | tf_op jit(solution)/shard_map/ppermute | solution.py:63
  439.5 38.3 %all-to-all-start.8 = ((bf16[4,128,2048]{2,1,0:T(8,128)(2,1)}), bf16[4,128,2048]{2,1,0:T(8,128)(2,1)}, u32[]{:S(2)}, u32[]{:S(2)}) async-start(bf16[4,128,2048]{2,1,0:T(8,128)(2,1)} %bitcast.220), calls=%async_computation.8 | async-start | bytes 4194304 | tf_op jit(solution)/shard_map/all_to_all | solution.py:95
  476.6 48.9 %collective-permute-start.40 = (bf16[384,2048]{1,0:T(8,128)(2,1)}, bf16[384,2048]{1,0:T(8,128)(2,1)}, u32[]{:S(2)}, u32[]{:S(2)}) collective-permute-start(bf16[384,2048]{1,0:T(8,128)(2,1)} %fusion.6), channel_id=1, source_target_pairs={{0,64},{1,65},{2,66},{3,67},{4,68},{5,69},{6,70},{7,71},{8,72},{9,... | collective-permute-start | bytes 4718600 | tf_op jit(solution)/shard_map/ppermute | solution.py:63
  536.2 59.2 %collective-permute-start.22 = (bf16[512,2048]{1,0:T(8,128)(2,1)}, bf16[512,2048]{1,0:T(8,128)(2,1)}, u32[]{:S(2)}, u32[]{:S(2)}) collective-permute-start(bf16[512,2048]{1,0:T(8,128)(2,1)} %slice.481), channel_id=1, source_target_pairs={{0,1},{1,0},{2,3},{3,2},{4,5},{5,4},{6,7},{7,6},{8,9},{9,8},{10,11... | collective-permute-start | bytes 6291464 | tf_op jit(solution)/shard_map/ppermute | solution.py:63
  600.1 44.1 %all-to-all-start.12 = ((bf16[4,128,2048]{2,1,0:T(8,128)(2,1)}), bf16[4,128,2048]{2,1,0:T(8,128)(2,1)}, u32[]{:S(2)}, u32[]{:S(2)}) async-start(bf16[4,128,2048]{2,1,0:T(8,128)(2,1)} %bitcast.219), calls=%async_computation.12 | async-start | bytes 4194304 | tf_op jit(solution)/shard_map/all_to_all | solution.py:95
  (104 other events, 1185.1 us)
